TPU v7x, 512 devices: a whole 4x4x16 slice. The times are simulated.
512 devices in a mesh: layer: 8 (over y, core), feat: 16 (over z_hi, x), width: 4 (over z_lo).
Axes of the slice: x: 4, y: 4, z: 16 (z_hi: 4, z_lo: 4; z = z_hi * 4 + z_lo), core: 2. Of those that a mesh axis runs over, the one named last changes fastest.
Arguments:
- resid: bfloat16 [2, 128, 2048], P(None, 'layer', 'width'), may hold values from -6 to 6
- enc_w: bfloat16 [2, 2048, 65536], P(None, 'width', ('layer', 'feat')), may hold values from -0.125 to 0.125
- enc_b: float32 [2, 65536], P(None, ('layer', 'feat')), may hold values from -3 to 3
- dec_w: float32 [3, 65536, 2048], P(None, ('layer', 'feat'), 'width'), may hold values from -0.09375 to 0.09375
- dec_b: float32 [2, 2048], P(None, 'width'), may hold values from -2 to 2
- target: float32 [2, 128, 2048], P(None, ('layer', 'feat'), 'width'), may hold values from -6 to 6
Outputs:
- recon: float32 [2, 128, 2048], P(None, ('layer', 'feat'), 'width')
- err: float32 [2, 128], P(None, ('layer', 'feat'))
All inputs are finite; a program needn't handle non-finite values.
Results may differ from a plain program's by a relative error of at most 0.00035.
Values may be sent and summed in bfloat16 or wider, within the bound.
A program may use at most 64 MiB of HBM per device.

v0:
```python
import jax
import jax.numpy as jnp
from jax import lax
from jax.sharding import PartitionSpec as P


def decode_rows(act, dec_w, target_idx):
    total = None
    for layer_idx in range(target_idx + 1):
        block = target_idx * (target_idx + 1) // 2 + layer_idx
        rows = act[layer_idx]
        term = jnp.dot(
            rows, dec_w[block], precision=lax.Precision.HIGHEST, preferred_element_type=jnp.float32
        )
        total = term if total is None else total + term
    return total


def per_device(resid, enc_w, enc_b, dec_w, dec_b, target):
    layers = resid.shape[0]
    gathered = lax.all_gather(resid, "layer", axis=1, tiled=True)
    tokens = gathered.shape[1]
    partial_pre = jnp.einsum("ltd,ldf->ltf", gathered, enc_w, preferred_element_type=jnp.float32)
    pre = lax.psum(partial_pre, "width")
    act = jnp.maximum(pre + enc_b[:, None, :], 0.0)
    own_rows = tokens // lax.axis_size(("layer", "feat"))
    pieces = []
    for target_idx in range(layers):

        def decode_single(start, count, target_idx=target_idx):
            return decode_rows(act, dec_w, target_idx)

        pieces.append(
            lax.psum_scatter(
                decode_single(jnp.int32(0), own_rows * lax.axis_size(("layer", "feat"))),
                ("layer", "feat"),
                scatter_dimension=0,
                tiled=True,
            )
        )
    summed = jnp.stack(pieces, 0)
    recon = summed + dec_b[:, None, :]
    diff = recon - target
    sq_error, sq_target = lax.psum(
        (jnp.sum(diff * diff, axis=2), jnp.sum(target * target, axis=2)), "width"
    )
    err = sq_error / (sq_target + 1e-06)
    return (recon, err)


def solution(mesh):
    in_specs = (
        P(None, "layer", "width"),
        P(None, "width", ("layer", "feat")),
        P(None, ("layer", "feat")),
        P(None, ("layer", "feat"), "width"),
        P(None, "width"),
        P(None, ("layer", "feat"), "width"),
    )
    out_specs = (P(None, ("layer", "feat"), "width"), P(None, ("layer", "feat")))
    return jax.shard_map(
        per_device, mesh=mesh, in_specs=in_specs, out_specs=out_specs, check_vma=False
    )
```

profile of v0, /device:TPU:32, one launch (start us, length us, event | category | flops | bytes accessed | tf_op | source)
XLA Modules:
  0.0 1588.4 jit_solution(10520074433764686368)
XLA Ops:
  7.2 0.0 copy-start
  7.2 0.0 all-reduce.7.cloned.1.call-start
  7.2 13.7 all_gather.3
  20.9 0.0 copy-done
  20.9 1.1 fusion.12
  22.1 0.0 all-reduce.7.cloned.1.call-update
  22.1 0.0 copy-start.1
  22.1 0.0 copy-start.2
  22.1 0.0 all-reduce.9.cloned.1.call-start
  22.2 64.1 %all-reduce.7.cloned.1.call-done = f32[2,128,512]{2,1,0:T(8,128)} async-done(((f32[2,128,512]{2,1,0:T(8,128)}), f32[2,128,512]{2,1,0:T(8,128)}) %all-reduce.7.cloned.1.call-update) | async-done | bytes 524304 | tf_op jit(solution)/shard_map/psum | solution.py:24
  86.2 1.1 add_maximum_fusion
  87.3 1.9 fusion.1
  89.3 2.7 fusion.3
  91.9 2.6 convolution_add_fusion
  94.6 0.0 all-reduce.9.cloned.1.call-update
  94.6 1.3 dynamic-slice
  95.9 0.0 copy-done.1
  95.9 0.1 multiply_reduce_fusion
  96.0 1473.3 %all-reduce.9.cloned.1.call-done = (f32[128,512]{1,0:T(8,128)}, f32[128,512]{1,0:T(8,128)}) async-done(((f32[128,512]{1,0:T(8,128)}, f32[128,512]{1,0:T(8,128)}), (f32[128,512]{1,0:T(8,128)}, f32[128,512]{1,0:T(8,128)})) %all-reduce.9.cloned.1.call-update) | async-done | bytes 524304
  1569.3 1.4 constant_dynamic-slice_fusion
  1570.7 0.0 copy-done.2
  1570.7 0.1 fusion.10
  1570.8 0.6 copy.11
  1571.4 9.7 all-reduce.3
  1581.1 0.5 add_divide_fusion
Async XLA Ops:
  7.2 13.8 copy-start
  7.2 79.0 %all-reduce.7.cloned.1.call-start = ((), (), s32[]{:S(2)}) async-start(), calls=%async_computation | async-start | bytes 1048576 | tf_op jit(solution)/shard_map/psum | solution.py:24
  22.1 73.8 %copy-start.1 = (f32[2,1,512]{2,1,0:T(1,128)S(1)}, f32[2,1,512]{2,1,0:T(1,128)}, u32[]{:S(2)}) copy-start(f32[2,1,512]{2,1,0:T(1,128)} %param.11) | copy-start | bytes 12292
  22.1 1548.6 %copy-start.2 = (f32[2,512]{1,0:T(2,128)S(1)}, f32[2,512]{1,0:T(2,128)}, u32[]{:S(2)}) copy-start(f32[2,512]{1,0:T(2,128)} %param.10) | copy-start | bytes 12292
  22.1 1547.2 %all-reduce.9.cloned.1.call-start = ((), (), s32[]{:S(2)}) async-start(), calls=%async_computation.1 | async-start | bytes 1048576
Sparse Core Ops, SparseCore 0:
  22.2 63.9 all-reduce.6
  94.7 1474.5 all-reduce.8
where the time goes:
time: 1590 us
  waiting for transfers between devices  1540 us (97%)
  blocking collectives  23.4 us (1%)
    unnamed x3, waiting for transfers between devices  1470 us
    psum x1, waiting for transfers between devices, per_device(): pre = lax.psum(partial_pre, 'width')  64.1 us
  transfers between devices with their start and end apart: 2, of which 2 were waited for; matrix products, arithmetic and copies ran while one was open for 0% of the time, Pallas kernels for 0%

commit v1 on v0

--- a/solution.py
+++ b/solution.py
@@ -21,7 +21,7 @@
     gathered = lax.all_gather(resid, "layer", axis=1, tiled=True)
     tokens = gathered.shape[1]
     partial_pre = jnp.einsum("ltd,ldf->ltf", gathered, enc_w, preferred_element_type=jnp.float32)
-    pre = lax.psum(partial_pre, "width")
+    pre = jnp.sum(lax.all_gather(partial_pre, "width"), axis=0)
     act = jnp.maximum(pre + enc_b[:, None, :], 0.0)
     own_rows = tokens // lax.axis_size(("layer", "feat"))
     pieces = []

time: 1590 us -> 1580 us (level)
    psum x1 -> x0, waiting for transfers between devices: 64.1 us -> none  [per_device(): pre = lax.psum(partial_pre, 'width')]
    all_gather x0 -> x1, waiting for transfers between devices: none -> 58 us  [per_device(): pre = jnp.sum(lax.all_gather(partial_pre, 'width'), axis=0)]
where the time goes in v1:
time: 1580 us
  waiting for transfers between devices  1530 us (97%)
  blocking collectives  23.4 us (1%)
    unnamed x3, waiting for transfers between devices  1470 us
    all_gather x1, waiting for transfers between devices, per_device(): pre = jnp.sum(lax.all_gather(partial_pre, 'width'), axis=0)  58 us
  transfers between devices with their start and end apart: 2, of which 2 were waited for; matrix products, arithmetic and copies ran while one was open for 0% of the time, Pallas kernels for 0%

profile of v1, /device:TPU:32, one launch (start us, length us, event | category | flops | bytes accessed | tf_op | source)
XLA Modules:
  0.0 1583.2 jit_solution(6761668942352303609)
XLA Ops:
  7.2 0.0 copy-start
  7.2 0.0 copy-start.2
  7.2 0.0 all-gather.3.cloned.1.call-start
  7.2 13.7 all_gather.9
  20.9 0.0 copy-done
  20.9 1.1 fusion.12
  22.0 0.0 all-gather.3.cloned.1.call-update
  22.1 0.0 all-reduce.6.cloned.1.call-start
  22.1 58.0 %all-gather.3.cloned.1.call-done = f32[8,128,512]{2,1,0:T(8,128)} async-done(((f32[2,128,512]{2,1,0:T(8,128)}), f32[8,128,512]{2,1,0:T(8,128)}) %all-gather.3.cloned.1.call-update) | async-done | bytes 2097168 | tf_op jit(solution)/shard_map/all_gather | solution.py:24
  80.2 1.9 reduce_sum.31
  82.0 0.0 copy-done.2
  82.0 0.0 copy-start.1
  82.0 0.0 copy-start.3
  82.1 0.1 add_maximum_fusion
  82.1 1.9 fusion.1
  84.1 2.6 fusion.3
  86.7 2.6 convolution_add_fusion
  89.4 0.0 all-reduce.6.cloned.1.call-update
  89.4 1.3 dynamic-slice
  90.7 0.0 copy-done.1
  90.7 0.1 multiply_reduce_fusion
  90.8 1473.3 %all-reduce.6.cloned.1.call-done = (f32[128,512]{1,0:T(8,128)}, f32[128,512]{1,0:T(8,128)}) async-done(((f32[128,512]{1,0:T(8,128)}, f32[128,512]{1,0:T(8,128)}), (f32[128,512]{1,0:T(8,128)}, f32[128,512]{1,0:T(8,128)})) %all-reduce.6.cloned.1.call-update) | async-done | bytes 524304
  1564.0 1.4 constant_dynamic-slice_fusion
  1565.4 0.0 copy-done.3
  1565.4 0.1 fusion.10
  1565.6 0.6 copy.11
  1566.2 9.7 all-reduce.3
  1575.8 0.5 add_divide_fusion
Async XLA Ops:
  7.2 13.8 copy-start
  7.2 74.8 %copy-start.2 = (f32[2,512]{1,0:T(2,128)S(1)}, f32[2,512]{1,0:T(2,128)}, u32[]{:S(2)}) copy-start(f32[2,512]{1,0:T(2,128)} %param.8) | copy-start | bytes 12292
  7.2 73.0 %all-gather.3.cloned.1.call-start = ((), (), s32[]{:S(2)}) async-start(), calls=%async_computation | async-start | bytes 2621440 | tf_op jit(solution)/shard_map/all_gather | solution.py:24
  22.1 1542.0 %all-reduce.6.cloned.1.call-start = ((), (), s32[]{:S(2)}) async-start(), calls=%async_computation.1 | async-start | bytes 1048576
  82.0 8.6 copy-start.1
  82.0 1483.4 %copy-start.3 = (f32[2,512]{1,0:T(2,128)S(1)}, f32[2,512]{1,0:T(2,128)}, u32[]{:S(2)}) copy-start(f32[2,512]{1,0:T(2,128)} %param.10) | copy-start | bytes 12292
Sparse Core Ops, SparseCore 0:
  22.2 57.9 all-gather.2
  89.5 1474.4 all-reduce.5
